TPU v7x, 32 devices: a whole 2x2x4 slice. The times are simulated.
32 devices in a mesh: ctx: 8 (over z, core), tp: 2 (over x), run: 2 (over y).
Axes of the slice: x: 2, y: 2, z: 4, core: 2. Of those that a mesh axis runs over, the one named last changes fastest.
Arguments:
- tokens: bfloat16 [4096, 5120], P(('run', 'ctx')), parts along dimension 0, may hold values from -28 to 28
- block_order: int32 [32], replicated, may hold values from 0 to 31, each once
- doc_lengths: int32 [16], replicated, may hold values from 1 to 512, 2048 in all
- patch_pos: int32 [512], P(('run', 'ctx')), parts along dimension 0, may hold values from 0 to 2047, as said below
- clean_rows: bfloat16 [512, 5120], P(('run', 'ctx')), parts along dimension 0, may hold values from -6 to 6
- w_query: bfloat16 [5120, 5120], P(None, 'tp'), may hold values from -0.078125 to 0.078125
- q_bias: bfloat16 [5120], P('tp'), may hold values from -3 to 3
- w_key: bfloat16 [5120, 1024], P(None, 'tp'), may hold values from -0.078125 to 0.078125
- k_bias: bfloat16 [1024], P('tp'), may hold values from -3 to 3
- w_value: bfloat16 [5120, 1024], P(None, 'tp'), may hold values from -0.078125 to 0.078125
- v_bias: bfloat16 [1024], P('tp'), may hold values from -3 to 3
Outputs:
- attended: bfloat16 [4096, 5120], P(('run', 'ctx'), 'tp'), parts along dimension 0
There are 2 independent parts, one for each index of `run`. A program takes and returns all parts, laid end to end along the dimension named above; an argument that names none is the same for every part. Nothing has to cross between parts.
Inputs may be any that keep to these rules, and one draw needn't show every extreme that they name: `block_order`: every block index appears exactly once. `doc_lengths`: the lengths sum to 2048 and the largest equals 512. `patch_pos`: the 256 positions are distinct positions of the sequence, the first and the last position among them.
All inputs are finite; a program needn't handle non-finite values.
Results may differ from a plain program's by a relative error of at most 0.0076.
Values may be sent and summed in bfloat16 or wider, within the bound.
A program may use at most 128 MiB of HBM per device.

v0:
```python
import jax
import jax.numpy as jnp
from jax import lax
from jax.sharding import PartitionSpec as P

HD = 128
BLOCK = 64


THETA = 1000000.0


def rotate(head_rows, offset):
    half = head_rows.shape[-1] // 2
    frequency = jnp.power(
        jnp.float32(THETA), -2.0 * jnp.arange(half, dtype=jnp.float32) / head_rows.shape[-1]
    )
    angles = offset.astype(jnp.float32)[:, None] * frequency[None, :]
    cosines = jnp.cos(angles)[:, None, :]
    sines = jnp.sin(angles)[:, None, :]
    first_half = head_rows[..., :half]
    second_half = head_rows[..., half:]
    return jnp.concatenate(
        [first_half * cosines - second_half * sines, second_half * cosines + first_half * sines],
        axis=-1,
    )


def project(source, weight, bias, offset, rotated):
    result = (
        jnp.dot(source, weight, preferred_element_type=jnp.float32)
        + bias.astype(jnp.float32)[None, :]
    )
    if rotated:
        result = rotate(result.reshape(source.shape[0], -1, HD), offset).reshape(
            source.shape[0], -1
        )
    return result.astype(jnp.bfloat16)


def slot_places(order, first_row, row_count):
    slots = first_row + jnp.arange(row_count, dtype=jnp.int32)
    owners = slots // BLOCK
    selector = owners[:, None] == jnp.arange(order.shape[0], dtype=jnp.int32)[None, :]
    picked = jnp.sum(jnp.where(selector, order[None, :], 0), axis=1)
    return picked * BLOCK + slots % BLOCK


def document_info(places, lengths):
    bounds = jnp.cumsum(lengths)
    passed = places[:, None] >= bounds[None, :]
    documents = jnp.sum(passed.astype(jnp.int32), axis=1)
    starts = jnp.sum(jnp.where(passed, lengths[None, :], 0), axis=1)
    return (documents, places - starts)


def match_patches(places, patch_places):
    matches = places[:, None] == patch_places[None, :]
    present = jnp.any(matches, axis=1)
    chosen = jnp.sum(
        jnp.where(matches, jnp.arange(patch_places.shape[0], dtype=jnp.int32)[None, :], 0), axis=1
    )
    return (present, chosen)


def body(
    tokens,
    block_order,
    doc_lengths,
    patch_pos,
    clean_rows,
    w_query,
    q_bias,
    w_key,
    k_bias,
    w_value,
    v_bias,
):
    local_rows = tokens.shape[0]
    first_row = lax.axis_index("ctx") * local_rows
    places = slot_places(block_order, first_row, local_rows)
    documents, offset = document_info(places, doc_lengths)
    key_heads = w_key.shape[1] // HD
    group_size = w_query.shape[1] // w_key.shape[1]
    gathered_rows, gathered_places = (
        lax.all_gather(clean_rows, "ctx", axis=0, tiled=True),
        lax.all_gather(patch_pos, "ctx", axis=0, tiled=True),
    )
    present, chosen = match_patches(places, gathered_places)
    patched = jnp.where(present[:, None], gathered_rows[chosen], tokens)
    query = project(patched, w_query, q_bias, offset, True)
    keys = project(patched, w_key, k_bias, offset, True)
    values = project(patched, w_value, v_bias, offset, False)
    grouped_query = query.reshape(local_rows, key_heads, group_size, HD)
    score_scale = HD ** (-0.5)

    def attend(running, block_keys, block_values, block_first):
        span_rows = block_keys.shape[0]
        key_places = slot_places(block_order, block_first, span_rows)
        key_documents = document_info(key_places, doc_lengths)[0]
        visible = (documents[:, None] == key_documents[None, :]) & (
            key_places[None, :] <= places[:, None]
        )
        peaks, totals, sums = running
        scores = (
            jnp.einsum(
                "tkgd,skd->tkgs",
                grouped_query,
                block_keys.reshape(span_rows, key_heads, HD),
                preferred_element_type=jnp.float32,
            )
            * score_scale
        )
        shown = visible[:, None, None, :]
        newest = jnp.maximum(peaks, jnp.max(jnp.where(shown, scores, -1e30), axis=-1))
        factor = jnp.exp(peaks - newest)
        weights = jnp.where(shown, jnp.exp(scores - newest[..., None]), 0.0)
        totals = totals * factor + jnp.sum(weights, axis=-1)
        sums = sums * factor[..., None] + jnp.einsum(
            "tkgs,skd->tkgd",
            weights.astype(jnp.bfloat16),
            block_values.reshape(span_rows, key_heads, HD),
            preferred_element_type=jnp.float32,
        )
        return (newest, totals, sums)

    initial = (
        jnp.full((local_rows, key_heads, group_size), -1e30, jnp.float32),
        jnp.zeros((local_rows, key_heads, group_size), jnp.float32),
        jnp.zeros((local_rows, key_heads, group_size, HD), jnp.float32),
    )
    shard_keys = lax.all_gather(keys, "ctx", axis=0, tiled=True)
    shard_values = lax.all_gather(values, "ctx", axis=0, tiled=True)
    total_rows = shard_keys.shape[0]
    span_rows = 512
    blocks_in = total_rows // span_rows

    def advance(previous, current):
        return (attend(previous, current[0], current[1], current[2]), None)

    begins = span_rows * jnp.arange(blocks_in, dtype=jnp.int32)
    stacked_keys = shard_keys.reshape(blocks_in, span_rows, shard_keys.shape[1])
    stacked_values = shard_values.reshape(blocks_in, span_rows, shard_values.shape[1])
    peaks, totals, sums = lax.scan(advance, initial, (stacked_keys, stacked_values, begins))[0]
    return (sums / totals[..., None]).reshape(local_rows, -1).astype(jnp.bfloat16)


def solution(mesh):
    in_specs = (
        P(("run", "ctx"), None),
        P(),
        P(),
        P(("run", "ctx")),
        P(("run", "ctx"), None),
        P(None, "tp"),
        P("tp"),
        P(None, "tp"),
        P("tp"),
        P(None, "tp"),
        P("tp"),
    )
    out_specs = P(("run", "ctx"), "tp")
    return jax.shard_map(body, mesh=mesh, in_specs=in_specs, out_specs=out_specs, check_vma=False)
```

profile of v0, /device:TPU:1, one launch (start us, length us, event | category | flops | bytes accessed | tf_op | source)
XLA Modules:
  0.0 176.5 jit_solution(1731406941072165080)
XLA Ops:
  10.7 8.4 %all-reduce = s32[256]{0:T(256)S(1)} all-reduce(s32[256]{0:T(256)S(1)} %dynamic-update-slice), channel_id=1, replica_groups=mesh['ctx'=8,'tp'=2,'run'=2] {'ctx'}, use_global_device_ids=true, to_apply=%add | all-reduce | flops 256 | bytes 2048
  20.4 25.0 %all-gather.4.cloned.1.call-done = bf16[256,5120]{1,0:T(8,128)(2,1)} async-done(((bf16[32,5120]{1,0:T(8,128)(2,1)}), bf16[256,5120]{1,0:T(8,128)(2,1)}) %all-gather.4.cloned.1.call-update) | async-done | bytes 2621456 | tf_op jit(solution)/shard_map/all_gather | solution.py:86
  45.4 6.8 %gather_fusion = bf16[256,5120]{1,0:T(8,128)(2,1)S(1)} fusion(bf16[256,5120]{1,0:T(8,128)(2,1)} %all-gather.4.cloned.1.call-done, s32[1024]{0:T(1024)S(1)} %pad_clamp_fusion), kind=kCustom, calls=%fused_computation | custom fusion | bytes 5243904 | tf_op jit(solution)/shard_map/gather | solution.py:90
  52.2 2.2 %broadcast_select_fusion = bf16[256,5120]{1,0:T(8,128)(2,1)S(1)} fusion(bf16[256,5120]{1,0:T(8,128)(2,1)S(1)} %gather_fusion, bf16[256,5120]{1,0:T(8,128)(2,1)} %param.13, pred[256]{0:T(512)(128)(4,1)S(1)} %compare_reduce_fusion), kind=kLoop, calls=%fused_computation.40 | loop fusion | flops 1310720 | bytes 7864576 | tf_op jit(solution)/shard_map/jit(_where)/select_n | solution.py:90
  55.9 2.2 %fusion.20 = bf16[256,512]{1,0:T(8,128)(2,1)} fusion(bf16[256,5120]{1,0:T(8,128)(2,1)S(1)} %broadcast_select_fusion, bf16[5120,512]{1,0:T(8,128)(2,1)S(1)} %copy-done.8, f32[512]{0:T(512)S(1)} %convert_element_type.56), kind=kOutput, calls=%fused_computation.46 | convolution fusion | flops 1342439424 | bytes 8128512 | tf_op jit(solution)/shard_map/dot_general | solution.py:31
  59.7 5.6 %convolution_add_fusion.2 = f32[256,512]{1,0:T(8,128)} fusion(bf16[256,5120]{1,0:T(8,128)(2,1)} %copy-done, bf16[5120,512]{1,0:T(8,128)(2,1)} %param.20, f32[512]{0:T(512)S(1)} %convert_element_type.51), kind=kOutput, calls=%fused_computation.45 | convolution fusion | flops 1342308352 | bytes 8390656 | tf_op jit(solution)/shard_map/dot_general | solution.py:31
  69.3 14.1 %convolution_add_fusion = f32[256,2560]{1,0:T(8,128)} fusion(bf16[256,5120]{1,0:T(8,128)(2,1)S(1)} %copy-done.1, bf16[5120,2560]{1,0:T(8,128)(2,1)} %param.18, f32[2560]{0:T(1024)S(1)} %convert_element_type.54), kind=kOutput, calls=%fused_computation.38 | convolution fusion | flops 6711541760 | bytes 31467520 | tf_op jit(solution)/shard_map/dot_general | solution.py:31
  83.4 2.2 %copy.37 = f32[256,2560]{0,1:T(8,128)S(1)} copy(f32[256,2560]{1,0:T(8,128)} %convolution_add_fusion) | data formatting | bytes 5242880 | tf_op jit(solution)/shard_map/add | solution.py:31
  86.9 29.9 %all-gather.6.cloned.1.call-done = bf16[2048,512]{1,0:T(8,128)(2,1)} async-done(((bf16[256,512]{1,0:T(8,128)(2,1)}), bf16[2048,512]{1,0:T(8,128)(2,1)}) %all-gather.6.cloned.1.call-update) | async-done | bytes 2097168 | tf_op jit(solution)/shard_map/all_gather | solution.py:132
  116.8 49.6 %while.17 = (s32[]{:T(128)}, f32[256,4,5]{0,2,1:T(8,128)S(1)}, f32[256,4,5]{0,2,1:T(8,128)S(1)}, f32[256,4,5,128]{0,3,2,1:T(8,128)}, s32[256]{0:T(256)S(1)}, /*i...) while((s32[]{:T(128)}, f32[256,4,5]{0,2,1:T(8,128)S(1)}, ...), condition=%wide.region_11.12_spmd.clone, body=%wide.region_6.11_spmd.clone.sunk | while | flops 1373486080 | bytes 65098152 | solution.py:144
  120.8 1.9 %fusion.48 = (f32[256,4,5]{0,2,1:T(8,128)S(1)}, f32[4,512,256,5]{2,1,3,0:T(8,128)S(1)}) fusion(pred[256,512]{0,1:T(8,128)(4,1)S(1)} %compare_and_fusion.2, bf16[512,4,128,1]{0,2,3,1:T(8,128)(2,1)S(1)} %bitcast.75, bf16[256,4,5,128]{3,0,2,1:T(8,128)(2,1)S(1)} %get-tuple-element.410), kind=kOutput, calls=%fused_computation.3.clone.1 | convolution fusion | flops 678947840 | bytes 12472320 | tf_op jit(solution)/shard_map/while/body/eval_jaxpr/tkgd,skd->tkgs/dot_general | solution.py:106
  122.7 2.1 %fusion.49 = f32[256,4,5]{0,2,1:T(8,128)S(1)} fusion(f32[4,512,256,5]{2,1,3,0:T(8,128)S(1)} %get-tuple-element.368, f32[256,4,5]{0,2,1:T(8,128)S(1)} %select_maximum_fusion.2, pred[256,512]{0,1:T(8,128)(4,1)S(1)} %compare_and_fusion.2), kind=kLoop, calls=%fused_computation.7.clone.1 | loop fusion | flops 10480640 | bytes 10657792 | tf_op jit(solution)/shard_map/while/body/eval_jaxpr/reduce_sum | solution.py:118
  124.9 2.8 %bitcast_add_fusion.2 = f32[256,4,5,128]{0,3,2,1:T(8,128)S(1)} fusion(f32[256,4,5,128]{0,3,2,1:T(8,128)S(1)} %copy-done.2, bf16[512,4,128,1]{0,2,3,1:T(8,128)(2,1)S(1)} %bitcast.76, f32[4,512,256,5]{2,1,3,0:T(8,128)S(1)} %get-tuple-element.368, f32[256,4,5]{0,2,1:T(8,128)S(1)} %select_maximum_fusion.2, pred[256,512]{0,1:T(8,128)(4,1)S(1)} %compare_and_fusion.2, ...), kind=kOutput, calls=%fused_computation.13.clone.1 | convolution fusion | flops 683540480 | bytes 16424961 | tf_op jit(solution)/shard_map/while/body/eval_jaxpr/tkgs,skd->tkgd/dot_general | solution.py:119
  133.2 1.9 %fusion.48 = (f32[256,4,5]{0,2,1:T(8,128)S(1)}, f32[4,512,256,5]{2,1,3,0:T(8,128)S(1)}) fusion(pred[256,512]{0,1:T(8,128)(4,1)S(1)} %compare_and_fusion.2, bf16[512,4,128,1]{0,2,3,1:T(8,128)(2,1)S(1)} %bitcast.75, bf16[256,4,5,128]{3,0,2,1:T(8,128)(2,1)S(1)} %get-tuple-element.410), kind=kOutput, calls=%fused_computation.3.clone.1 | convolution fusion | flops 678947840 | bytes 12472320 | tf_op jit(solution)/shard_map/while/body/eval_jaxpr/tkgd,skd->tkgs/dot_general | solution.py:106
  135.1 2.1 %fusion.49 = f32[256,4,5]{0,2,1:T(8,128)S(1)} fusion(f32[4,512,256,5]{2,1,3,0:T(8,128)S(1)} %get-tuple-element.368, f32[256,4,5]{0,2,1:T(8,128)S(1)} %select_maximum_fusion.2, pred[256,512]{0,1:T(8,128)(4,1)S(1)} %compare_and_fusion.2), kind=kLoop, calls=%fused_computation.7.clone.1 | loop fusion | flops 10480640 | bytes 10657792 | tf_op jit(solution)/shard_map/while/body/eval_jaxpr/reduce_sum | solution.py:118
  137.3 2.8 %bitcast_add_fusion.2 = f32[256,4,5,128]{0,3,2,1:T(8,128)S(1)} fusion(f32[256,4,5,128]{0,3,2,1:T(8,128)S(1)} %copy-done.2, bf16[512,4,128,1]{0,2,3,1:T(8,128)(2,1)S(1)} %bitcast.76, f32[4,512,256,5]{2,1,3,0:T(8,128)S(1)} %get-tuple-element.368, f32[256,4,5]{0,2,1:T(8,128)S(1)} %select_maximum_fusion.2, pred[256,512]{0,1:T(8,128)(4,1)S(1)} %compare_and_fusion.2, ...), kind=kOutput, calls=%fused_computation.13.clone.1 | convolution fusion | flops 683540480 | bytes 16424961 | tf_op jit(solution)/shard_map/while/body/eval_jaxpr/tkgs,skd->tkgd/dot_general | solution.py:119
  145.6 1.9 %fusion.48 = (f32[256,4,5]{0,2,1:T(8,128)S(1)}, f32[4,512,256,5]{2,1,3,0:T(8,128)S(1)}) fusion(pred[256,512]{0,1:T(8,128)(4,1)S(1)} %compare_and_fusion.2, bf16[512,4,128,1]{0,2,3,1:T(8,128)(2,1)S(1)} %bitcast.75, bf16[256,4,5,128]{3,0,2,1:T(8,128)(2,1)S(1)} %get-tuple-element.410), kind=kOutput, calls=%fused_computation.3.clone.1 | convolution fusion | flops 678947840 | bytes 12472320 | tf_op jit(solution)/shard_map/while/body/eval_jaxpr/tkgd,skd->tkgs/dot_general | solution.py:106
  147.5 2.1 %fusion.49 = f32[256,4,5]{0,2,1:T(8,128)S(1)} fusion(f32[4,512,256,5]{2,1,3,0:T(8,128)S(1)} %get-tuple-element.368, f32[256,4,5]{0,2,1:T(8,128)S(1)} %select_maximum_fusion.2, pred[256,512]{0,1:T(8,128)(4,1)S(1)} %compare_and_fusion.2), kind=kLoop, calls=%fused_computation.7.clone.1 | loop fusion | flops 10480640 | bytes 10657792 | tf_op jit(solution)/shard_map/while/body/eval_jaxpr/reduce_sum | solution.py:118
  149.7 2.8 %bitcast_add_fusion.2 = f32[256,4,5,128]{0,3,2,1:T(8,128)S(1)} fusion(f32[256,4,5,128]{0,3,2,1:T(8,128)S(1)} %copy-done.2, bf16[512,4,128,1]{0,2,3,1:T(8,128)(2,1)S(1)} %bitcast.76, f32[4,512,256,5]{2,1,3,0:T(8,128)S(1)} %get-tuple-element.368, f32[256,4,5]{0,2,1:T(8,128)S(1)} %select_maximum_fusion.2, pred[256,512]{0,1:T(8,128)(4,1)S(1)} %compare_and_fusion.2, ...), kind=kOutput, calls=%fused_computation.13.clone.1 | convolution fusion | flops 683540480 | bytes 16424961 | tf_op jit(solution)/shard_map/while/body/eval_jaxpr/tkgs,skd->tkgd/dot_general | solution.py:119
  158.0 1.9 %fusion.48 = (f32[256,4,5]{0,2,1:T(8,128)S(1)}, f32[4,512,256,5]{2,1,3,0:T(8,128)S(1)}) fusion(pred[256,512]{0,1:T(8,128)(4,1)S(1)} %compare_and_fusion.2, bf16[512,4,128,1]{0,2,3,1:T(8,128)(2,1)S(1)} %bitcast.75, bf16[256,4,5,128]{3,0,2,1:T(8,128)(2,1)S(1)} %get-tuple-element.410), kind=kOutput, calls=%fused_computation.3.clone.1 | convolution fusion | flops 678947840 | bytes 12472320 | tf_op jit(solution)/shard_map/while/body/eval_jaxpr/tkgd,skd->tkgs/dot_general | solution.py:106
  159.9 2.1 %fusion.49 = f32[256,4,5]{0,2,1:T(8,128)S(1)} fusion(f32[4,512,256,5]{2,1,3,0:T(8,128)S(1)} %get-tuple-element.368, f32[256,4,5]{0,2,1:T(8,128)S(1)} %select_maximum_fusion.2, pred[256,512]{0,1:T(8,128)(4,1)S(1)} %compare_and_fusion.2), kind=kLoop, calls=%fused_computation.7.clone.1 | loop fusion | flops 10480640 | bytes 10657792 | tf_op jit(solution)/shard_map/while/body/eval_jaxpr/reduce_sum | solution.py:118
  162.1 2.8 %bitcast_add_fusion.2 = f32[256,4,5,128]{0,3,2,1:T(8,128)S(1)} fusion(f32[256,4,5,128]{0,3,2,1:T(8,128)S(1)} %copy-done.2, bf16[512,4,128,1]{0,2,3,1:T(8,128)(2,1)S(1)} %bitcast.76, f32[4,512,256,5]{2,1,3,0:T(8,128)S(1)} %get-tuple-element.368, f32[256,4,5]{0,2,1:T(8,128)S(1)} %select_maximum_fusion.2, pred[256,512]{0,1:T(8,128)(4,1)S(1)} %compare_and_fusion.2, ...), kind=kOutput, calls=%fused_computation.13.clone.1 | convolution fusion | flops 683540480 | bytes 16424961 | tf_op jit(solution)/shard_map/while/body/eval_jaxpr/tkgs,skd->tkgd/dot_general | solution.py:119
  166.4 2.0 %divide_convert_fusion = bf16[256,4,5,128]{0,3,2,1:T(8,128)(2,1)S(1)} fusion(f32[256,4,5,128]{0,3,2,1:T(8,128)} %get-tuple-element.160, f32[256,4,5]{0,2,1:T(8,128)S(1)} %get-tuple-element.161), kind=kLoop, calls=%fused_computation.39 | loop fusion | flops 1310720 | bytes 3952640 | tf_op jit(solution)/shard_map/convert_element_type | solution.py:145
  168.4 1.6 copy.41
  (116 shorter events, 34.9 us)
Async XLA Ops:
  6.5 38.8 %all-gather.4.cloned.1.call-start = ((), (), s32[]{:S(2)}) async-start(), calls=%async_computation | async-start | bytes 2949120 | tf_op jit(solution)/shard_map/all_gather | solution.py:86
  7.3 79.6 %all-gather.8.cloned.1.call-start = ((), (), s32[]{:S(2)}) async-start(), calls=%async_computation.2 | async-start | bytes 2359296 | tf_op jit(solution)/shard_map/all_gather | solution.py:133
  52.1 3.8 %copy-start.8 = (bf16[5120,512]{1,0:T(8,128)(2,1)S(1)}, bf16[5120,512]{1,0:T(8,128)(2,1)}, u32[]{:S(2)}) copy-start(bf16[5120,512]{1,0:T(8,128)(2,1)} %param.22) | copy-start | bytes 15728644
  54.4 1.5 copy-start
  55.9 2.3 %copy-start.7 = (s32[16]{0:T(128)S(1)}, s32[16]{0:T(128)}, u32[]{:S(2)}) copy-start(s32[16]{0:T(128)} %param.15) | copy-start | bytes 196
  55.9 2.5 %copy-start.6 = (bf16[512]{0:T(512)(128)(2,1)S(1)}, bf16[512]{0:T(512)(128)(2,1)}, u32[]{:S(2)}) copy-start(bf16[512]{0:T(512)(128)(2,1)} %param.21) | copy-start | bytes 3076
  58.2 58.6 %all-gather.6.cloned.1.call-start = ((), (), s32[]{:S(2)}) async-start(), calls=%async_computation.1 | async-start | bytes 2359296 | tf_op jit(solution)/shard_map/all_gather | solution.py:132
  65.3 3.9 %copy-start.5 = (bf16[2560]{0:T(1024)(128)(2,1)S(1)}, bf16[2560]{0:T(1024)(128)(2,1)}, u32[]{:S(2)}) copy-start(bf16[2560]{0:T(1024)(128)(2,1)} %param.19) | copy-start | bytes 15364
  65.3 4.0 %copy-start.1 = (bf16[256,5120]{1,0:T(8,128)(2,1)S(1)}, bf16[256,5120]{1,0:T(8,128)(2,1)}, u32[]{:S(2)}) copy-start(bf16[256,5120]{1,0:T(8,128)(2,1)} %copy-done) | copy-start | bytes 7864324
  86.0 30.8 %copy-start.4 = (s32[32]{0:T(128)S(1)}, s32[32]{0:T(128)}, u32[]{:S(2)}) copy-start(s32[32]{0:T(128)} %param.14) | copy-start | bytes 388
  122.7 2.2 %copy-start.2 = (f32[256,4,5,128]{0,3,2,1:T(8,128)S(1)}, f32[256,4,5,128]{0,3,2,1:T(8,128)}, u32[]{:S(2)}) copy-start(f32[256,4,5,128]{0,3,2,1:T(8,128)} %get-tuple-element.389) | copy-start | bytes 7864324 | tf_op jit(solution)/shard_map/while
  127.7 1.5 copy-start.3
  135.1 2.2 %copy-start.2 = (f32[256,4,5,128]{0,3,2,1:T(8,128)S(1)}, f32[256,4,5,128]{0,3,2,1:T(8,128)}, u32[]{:S(2)}) copy-start(f32[256,4,5,128]{0,3,2,1:T(8,128)} %get-tuple-element.389) | copy-start | bytes 7864324 | tf_op jit(solution)/shard_map/while
  140.1 1.5 copy-start.3
  147.5 2.2 %copy-start.2 = (f32[256,4,5,128]{0,3,2,1:T(8,128)S(1)}, f32[256,4,5,128]{0,3,2,1:T(8,128)}, u32[]{:S(2)}) copy-start(f32[256,4,5,128]{0,3,2,1:T(8,128)} %get-tuple-element.389) | copy-start | bytes 7864324 | tf_op jit(solution)/shard_map/while
  152.5 1.5 copy-start.3
  159.9 2.2 %copy-start.2 = (f32[256,4,5,128]{0,3,2,1:T(8,128)S(1)}, f32[256,4,5,128]{0,3,2,1:T(8,128)}, u32[]{:S(2)}) copy-start(f32[256,4,5,128]{0,3,2,1:T(8,128)} %get-tuple-element.389) | copy-start | bytes 7864324 | tf_op jit(solution)/shard_map/while
  164.9 1.5 copy-start.3
Sparse Core Ops, SparseCore 0:
  9.0 36.3 all-gather.3
  58.3 28.2 all-gather.7
  88.2 28.5 all-gather.5
where the time goes:
time: 177 us
  waiting for transfers between devices  55.7 us (31%)
  matrix products  40.6 us (23%)
  local copies, waits for them, and re-layouts  33 us (19%)
  other arithmetic  24.4 us (14%)
  between operations  14 us (8%)
  blocking collectives  8.45 us (5%)
    all_gather x1, waiting for transfers between devices, body(): shard_keys = lax.all_gather(keys, 'ctx', axis=0, tiled=True)  29.9 us
    all_gather x1, waiting for transfers between devices, body(): lax.all_gather(clean_rows, 'ctx', axis=0, tiled=True)  25 us
    dot_general x3, matrix products, project(): jnp.dot(source, weight, preferred_element_type=jnp.float32)  21.9 us
    dot_general x4, matrix products, attend(): jnp.einsum('tkgs,skd->tkgd', weights.astype(jnp.bfloat16), block_values.r...  11.1 us
    dynamic_slice x16, local copies, waits for them, and re-layouts, body(): lax.scan(advance, initial, (stacked_keys, stacked_values, begins))[0]  9.13 us
    reduce_sum x4, other arithmetic, attend(): totals = totals * factor + jnp.sum(weights, axis=-1)  8.52 us
    unnamed x1, blocking collectives  8.45 us
    dot_general x4, matrix products, attend(): jnp.einsum('tkgd,skd->tkgs', grouped_query, block_keys.reshape(span_rows,...  7.53 us
  transfers between devices with their start and end apart: 3, of which 2 were waited for; matrix products, arithmetic and copies ran while one was open for 18% of the time, Pallas kernels for 0%

commit v1 on v0

--- a/solution.py
+++ b/solution.py
@@ -47,7 +47,8 @@
 
 
 def document_info(places, lengths):
-    bounds = jnp.cumsum(lengths)
+    index = jnp.arange(lengths.shape[0], dtype=jnp.int32)
+    bounds = jnp.sum(jnp.where(index[:, None] <= index[None, :], lengths[:, None], 0), axis=0)
     passed = places[:, None] >= bounds[None, :]
     documents = jnp.sum(passed.astype(jnp.int32), axis=1)
     starts = jnp.sum(jnp.where(passed, lengths[None, :], 0), axis=1)

time: 177 us -> 178 us (level)
  no operation moved by 1% of the time
where the time goes in v1:
time: 178 us; the launch traced here: 177 us
  waiting for transfers between devices  55.7 us (31%)
  matrix products  40.6 us (23%)
  local copies, waits for them, and re-layouts  33 us (19%)
  other arithmetic  24.6 us (14%)
  between operations  14 us (8%)
  blocking collectives  8.45 us (5%)
    all_gather x1, waiting for transfers between devices, body(): shard_keys = lax.all_gather(keys, 'ctx', axis=0, tiled=True)  30 us
    all_gather x1, waiting for transfers between devices, body(): lax.all_gather(clean_rows, 'ctx', axis=0, tiled=True)  25 us
    dot_general x3, matrix products, project(): jnp.dot(source, weight, preferred_element_type=jnp.float32)  21.9 us
    dot_general x4, matrix products, attend(): jnp.einsum('tkgs,skd->tkgd', weights.astype(jnp.bfloat16), block_values.r...  11.1 us
    dynamic_slice x16, local copies, waits for them, and re-layouts, body(): lax.scan(advance, initial, (stacked_keys, stacked_values, begins))[0]  9.13 us
    reduce_sum x4, other arithmetic, attend(): totals = totals * factor + jnp.sum(weights, axis=-1)  8.52 us
    unnamed x1, blocking collectives  8.45 us
    dot_general x4, matrix products, attend(): jnp.einsum('tkgd,skd->tkgs', grouped_query, block_keys.reshape(span_rows,...  7.52 us
  transfers between devices with their start and end apart: 3, of which 2 were waited for; matrix products, arithmetic and copies ran while one was open for 18% of the time, Pallas kernels for 0%

profile of v1, /device:TPU:1, one launch (start us, length us, event | category | flops | bytes accessed | tf_op | source)
XLA Modules:
  0.0 176.9 jit_solution(6808619034733549920)
XLA Ops:
  10.7 8.4 %all-reduce = s32[256]{0:T(256)S(1)} all-reduce(s32[256]{0:T(256)S(1)} %dynamic-update-slice), channel_id=1, replica_groups=mesh['ctx'=8,'tp'=2,'run'=2] {'ctx'}, use_global_device_ids=true, to_apply=%add | all-reduce | flops 256 | bytes 2048
  20.4 25.0 %all-gather.4.cloned.1.call-done = bf16[256,5120]{1,0:T(8,128)(2,1)} async-done(((bf16[32,5120]{1,0:T(8,128)(2,1)}), bf16[256,5120]{1,0:T(8,128)(2,1)}) %all-gather.4.cloned.1.call-update) | async-done | bytes 2621456 | tf_op jit(solution)/shard_map/all_gather | solution.py:87
  45.4 6.8 %gather_fusion = bf16[256,5120]{1,0:T(8,128)(2,1)S(1)} fusion(bf16[256,5120]{1,0:T(8,128)(2,1)} %all-gather.4.cloned.1.call-done, s32[1024]{0:T(1024)S(1)} %pad_clamp_fusion), kind=kCustom, calls=%fused_computation | custom fusion | bytes 5243904 | tf_op jit(solution)/shard_map/gather | solution.py:91
  52.2 2.2 %broadcast_select_fusion = bf16[256,5120]{1,0:T(8,128)(2,1)S(1)} fusion(bf16[256,5120]{1,0:T(8,128)(2,1)S(1)} %gather_fusion, bf16[256,5120]{1,0:T(8,128)(2,1)} %param.13, pred[256]{0:T(512)(128)(4,1)S(1)} %compare_reduce_fusion), kind=kLoop, calls=%fused_computation.42 | loop fusion | flops 1310720 | bytes 7864576 | tf_op jit(solution)/shard_map/jit(_where)/select_n | solution.py:91
  55.9 2.2 %fusion.20 = bf16[256,512]{1,0:T(8,128)(2,1)} fusion(bf16[256,5120]{1,0:T(8,128)(2,1)S(1)} %broadcast_select_fusion, bf16[5120,512]{1,0:T(8,128)(2,1)S(1)} %copy-done.8, f32[512]{0:T(512)S(1)} %convert_element_type.56), kind=kOutput, calls=%fused_computation.48 | convolution fusion | flops 1342439424 | bytes 8128512 | tf_op jit(solution)/shard_map/dot_general | solution.py:31
  59.6 5.6 %convolution_add_fusion.2 = f32[256,512]{1,0:T(8,128)} fusion(bf16[256,5120]{1,0:T(8,128)(2,1)} %copy-done, bf16[5120,512]{1,0:T(8,128)(2,1)} %param.20, f32[512]{0:T(512)S(1)} %convert_element_type.51), kind=kOutput, calls=%fused_computation.47 | convolution fusion | flops 1342308352 | bytes 8390656 | tf_op jit(solution)/shard_map/dot_general | solution.py:31
  69.2 14.1 %convolution_add_fusion = f32[256,2560]{1,0:T(8,128)} fusion(bf16[256,5120]{1,0:T(8,128)(2,1)S(1)} %copy-done.1, bf16[5120,2560]{1,0:T(8,128)(2,1)} %param.18, f32[2560]{0:T(1024)S(1)} %convert_element_type.54), kind=kOutput, calls=%fused_computation.40 | convolution fusion | flops 6711541760 | bytes 31467520 | tf_op jit(solution)/shard_map/dot_general | solution.py:31
  83.3 2.2 %copy.37 = f32[256,2560]{0,1:T(8,128)S(1)} copy(f32[256,2560]{1,0:T(8,128)} %convolution_add_fusion) | data formatting | bytes 5242880 | tf_op jit(solution)/shard_map/add | solution.py:31
  86.8 30.0 %all-gather.6.cloned.1.call-done = bf16[2048,512]{1,0:T(8,128)(2,1)} async-done(((bf16[256,512]{1,0:T(8,128)(2,1)}), bf16[2048,512]{1,0:T(8,128)(2,1)}) %all-gather.6.cloned.1.call-update) | async-done | bytes 2097168 | tf_op jit(solution)/shard_map/all_gather | solution.py:133
  116.8 49.9 %while.17 = (s32[]{:T(128)}, f32[256,4,5]{0,2,1:T(8,128)S(1)}, f32[256,4,5]{0,2,1:T(8,128)S(1)}, f32[256,4,5,128]{0,3,2,1:T(8,128)}, s32[256]{0:T(256)S(1)}, /*i...) while((s32[]{:T(128)}, f32[256,4,5]{0,2,1:T(8,128)S(1)}, ...), condition=%wide.region_12.13_spmd.clone, body=%wide.region_6.12_spmd.clone.sunk | while | flops 1373486848 | bytes 65098280 | solution.py:145
  120.9 1.9 %fusion.48 = (f32[256,4,5]{0,2,1:T(8,128)S(1)}, f32[4,512,256,5]{2,1,3,0:T(8,128)S(1)}) fusion(pred[256,512]{0,1:T(8,128)(4,1)S(1)} %compare_and_fusion.2, bf16[512,4,128,1]{0,2,3,1:T(8,128)(2,1)S(1)} %bitcast.70, bf16[256,4,5,128]{3,0,2,1:T(8,128)(2,1)S(1)} %get-tuple-element.408), kind=kOutput, calls=%fused_computation.3.clone.1 | convolution fusion | flops 678947840 | bytes 12472320 | tf_op jit(solution)/shard_map/while/body/eval_jaxpr/tkgd,skd->tkgs/dot_general | solution.py:107
  122.8 2.1 %fusion.49 = f32[256,4,5]{0,2,1:T(8,128)S(1)} fusion(f32[4,512,256,5]{2,1,3,0:T(8,128)S(1)} %get-tuple-element.366, f32[256,4,5]{0,2,1:T(8,128)S(1)} %select_maximum_fusion.2, pred[256,512]{0,1:T(8,128)(4,1)S(1)} %compare_and_fusion.2), kind=kLoop, calls=%fused_computation.7.clone.1 | loop fusion | flops 10480640 | bytes 10657792 | tf_op jit(solution)/shard_map/while/body/eval_jaxpr/reduce_sum | solution.py:119
  125.0 2.8 %bitcast_add_fusion.2 = f32[256,4,5,128]{0,3,2,1:T(8,128)S(1)} fusion(f32[256,4,5,128]{0,3,2,1:T(8,128)S(1)} %copy-done.2, bf16[512,4,128,1]{0,2,3,1:T(8,128)(2,1)S(1)} %bitcast.71, f32[4,512,256,5]{2,1,3,0:T(8,128)S(1)} %get-tuple-element.366, f32[256,4,5]{0,2,1:T(8,128)S(1)} %select_maximum_fusion.2, pred[256,512]{0,1:T(8,128)(4,1)S(1)} %compare_and_fusion.2, ...), kind=kOutput, calls=%fused_computation.13.clone.1 | convolution fusion | flops 683540480 | bytes 16424961 | tf_op jit(solution)/shard_map/while/body/eval_jaxpr/tkgs,skd->tkgd/dot_general | solution.py:120
  133.4 1.9 %fusion.48 = (f32[256,4,5]{0,2,1:T(8,128)S(1)}, f32[4,512,256,5]{2,1,3,0:T(8,128)S(1)}) fusion(pred[256,512]{0,1:T(8,128)(4,1)S(1)} %compare_and_fusion.2, bf16[512,4,128,1]{0,2,3,1:T(8,128)(2,1)S(1)} %bitcast.70, bf16[256,4,5,128]{3,0,2,1:T(8,128)(2,1)S(1)} %get-tuple-element.408), kind=kOutput, calls=%fused_computation.3.clone.1 | convolution fusion | flops 678947840 | bytes 12472320 | tf_op jit(solution)/shard_map/while/body/eval_jaxpr/tkgd,skd->tkgs/dot_general | solution.py:107
  135.3 2.1 %fusion.49 = f32[256,4,5]{0,2,1:T(8,128)S(1)} fusion(f32[4,512,256,5]{2,1,3,0:T(8,128)S(1)} %get-tuple-element.366, f32[256,4,5]{0,2,1:T(8,128)S(1)} %select_maximum_fusion.2, pred[256,512]{0,1:T(8,128)(4,1)S(1)} %compare_and_fusion.2), kind=kLoop, calls=%fused_computation.7.clone.1 | loop fusion | flops 10480640 | bytes 10657792 | tf_op jit(solution)/shard_map/while/body/eval_jaxpr/reduce_sum | solution.py:119
  137.5 2.8 %bitcast_add_fusion.2 = f32[256,4,5,128]{0,3,2,1:T(8,128)S(1)} fusion(f32[256,4,5,128]{0,3,2,1:T(8,128)S(1)} %copy-done.2, bf16[512,4,128,1]{0,2,3,1:T(8,128)(2,1)S(1)} %bitcast.71, f32[4,512,256,5]{2,1,3,0:T(8,128)S(1)} %get-tuple-element.366, f32[256,4,5]{0,2,1:T(8,128)S(1)} %select_maximum_fusion.2, pred[256,512]{0,1:T(8,128)(4,1)S(1)} %compare_and_fusion.2, ...), kind=kOutput, calls=%fused_computation.13.clone.1 | convolution fusion | flops 683540480 | bytes 16424961 | tf_op jit(solution)/shard_map/while/body/eval_jaxpr/tkgs,skd->tkgd/dot_general | solution.py:120
  145.8 1.9 %fusion.48 = (f32[256,4,5]{0,2,1:T(8,128)S(1)}, f32[4,512,256,5]{2,1,3,0:T(8,128)S(1)}) fusion(pred[256,512]{0,1:T(8,128)(4,1)S(1)} %compare_and_fusion.2, bf16[512,4,128,1]{0,2,3,1:T(8,128)(2,1)S(1)} %bitcast.70, bf16[256,4,5,128]{3,0,2,1:T(8,128)(2,1)S(1)} %get-tuple-element.408), kind=kOutput, calls=%fused_computation.3.clone.1 | convolution fusion | flops 678947840 | bytes 12472320 | tf_op jit(solution)/shard_map/while/body/eval_jaxpr/tkgd,skd->tkgs/dot_general | solution.py:107
  147.8 2.1 %fusion.49 = f32[256,4,5]{0,2,1:T(8,128)S(1)} fusion(f32[4,512,256,5]{2,1,3,0:T(8,128)S(1)} %get-tuple-element.366, f32[256,4,5]{0,2,1:T(8,128)S(1)} %select_maximum_fusion.2, pred[256,512]{0,1:T(8,128)(4,1)S(1)} %compare_and_fusion.2), kind=kLoop, calls=%fused_computation.7.clone.1 | loop fusion | flops 10480640 | bytes 10657792 | tf_op jit(solution)/shard_map/while/body/eval_jaxpr/reduce_sum | solution.py:119
  149.9 2.8 %bitcast_add_fusion.2 = f32[256,4,5,128]{0,3,2,1:T(8,128)S(1)} fusion(f32[256,4,5,128]{0,3,2,1:T(8,128)S(1)} %copy-done.2, bf16[512,4,128,1]{0,2,3,1:T(8,128)(2,1)S(1)} %bitcast.71, f32[4,512,256,5]{2,1,3,0:T(8,128)S(1)} %get-tuple-element.366, f32[256,4,5]{0,2,1:T(8,128)S(1)} %select_maximum_fusion.2, pred[256,512]{0,1:T(8,128)(4,1)S(1)} %compare_and_fusion.2, ...), kind=kOutput, calls=%fused_computation.13.clone.1 | convolution fusion | flops 683540480 | bytes 16424961 | tf_op jit(solution)/shard_map/while/body/eval_jaxpr/tkgs,skd->tkgd/dot_general | solution.py:120
  158.3 1.9 %fusion.48 = (f32[256,4,5]{0,2,1:T(8,128)S(1)}, f32[4,512,256,5]{2,1,3,0:T(8,128)S(1)}) fusion(pred[256,512]{0,1:T(8,128)(4,1)S(1)} %compare_and_fusion.2, bf16[512,4,128,1]{0,2,3,1:T(8,128)(2,1)S(1)} %bitcast.70, bf16[256,4,5,128]{3,0,2,1:T(8,128)(2,1)S(1)} %get-tuple-element.408), kind=kOutput, calls=%fused_computation.3.clone.1 | convolution fusion | flops 678947840 | bytes 12472320 | tf_op jit(solution)/shard_map/while/body/eval_jaxpr/tkgd,skd->tkgs/dot_general | solution.py:107
  160.2 2.1 %fusion.49 = f32[256,4,5]{0,2,1:T(8,128)S(1)} fusion(f32[4,512,256,5]{2,1,3,0:T(8,128)S(1)} %get-tuple-element.366, f32[256,4,5]{0,2,1:T(8,128)S(1)} %select_maximum_fusion.2, pred[256,512]{0,1:T(8,128)(4,1)S(1)} %compare_and_fusion.2), kind=kLoop, calls=%fused_computation.7.clone.1 | loop fusion | flops 10480640 | bytes 10657792 | tf_op jit(solution)/shard_map/while/body/eval_jaxpr/reduce_sum | solution.py:119
  162.4 2.8 %bitcast_add_fusion.2 = f32[256,4,5,128]{0,3,2,1:T(8,128)S(1)} fusion(f32[256,4,5,128]{0,3,2,1:T(8,128)S(1)} %copy-done.2, bf16[512,4,128,1]{0,2,3,1:T(8,128)(2,1)S(1)} %bitcast.71, f32[4,512,256,5]{2,1,3,0:T(8,128)S(1)} %get-tuple-element.366, f32[256,4,5]{0,2,1:T(8,128)S(1)} %select_maximum_fusion.2, pred[256,512]{0,1:T(8,128)(4,1)S(1)} %compare_and_fusion.2, ...), kind=kOutput, calls=%fused_computation.13.clone.1 | convolution fusion | flops 683540480 | bytes 16424961 | tf_op jit(solution)/shard_map/while/body/eval_jaxpr/tkgs,skd->tkgd/dot_general | solution.py:120
  166.7 2.0 %divide_convert_fusion = bf16[256,4,5,128]{0,3,2,1:T(8,128)(2,1)S(1)} fusion(f32[256,4,5,128]{0,3,2,1:T(8,128)} %get-tuple-element.158, f32[256,4,5]{0,2,1:T(8,128)S(1)} %get-tuple-element.159), kind=kLoop, calls=%fused_computation.41 | loop fusion | flops 1310720 | bytes 3952640 | tf_op jit(solution)/shard_map/convert_element_type | solution.py:146
  168.7 1.6 copy.41
  (120 shorter events, 35.2 us)
Async XLA Ops:
  6.5 38.8 %all-gather.4.cloned.1.call-start = ((), (), s32[]{:S(2)}) async-start(), calls=%async_computation | async-start | bytes 2949120 | tf_op jit(solution)/shard_map/all_gather | solution.py:87
  7.3 79.5 %all-gather.8.cloned.1.call-start = ((), (), s32[]{:S(2)}) async-start(), calls=%async_computation.2 | async-start | bytes 2359296 | tf_op jit(solution)/shard_map/all_gather | solution.py:134
  52.1 3.8 %copy-start.8 = (bf16[5120,512]{1,0:T(8,128)(2,1)S(1)}, bf16[5120,512]{1,0:T(8,128)(2,1)}, u32[]{:S(2)}) copy-start(bf16[5120,512]{1,0:T(8,128)(2,1)} %param.22) | copy-start | bytes 15728644
  54.4 1.5 copy-start
  55.9 2.3 %copy-start.6 = (bf16[512]{0:T(512)(128)(2,1)S(1)}, bf16[512]{0:T(512)(128)(2,1)}, u32[]{:S(2)}) copy-start(bf16[512]{0:T(512)(128)(2,1)} %param.21) | copy-start | bytes 3076
  55.9 2.3 %copy-start.7 = (s32[16]{0:T(128)S(1)}, s32[16]{0:T(128)}, u32[]{:S(2)}) copy-start(s32[16]{0:T(128)} %param.15) | copy-start | bytes 196
  58.2 58.6 %all-gather.6.cloned.1.call-start = ((), (), s32[]{:S(2)}) async-start(), calls=%async_computation.1 | async-start | bytes 2359296 | tf_op jit(solution)/shard_map/all_gather | solution.py:133
  65.2 3.9 %copy-start.5 = (bf16[2560]{0:T(1024)(128)(2,1)S(1)}, bf16[2560]{0:T(1024)(128)(2,1)}, u32[]{:S(2)}) copy-start(bf16[2560]{0:T(1024)(128)(2,1)} %param.19) | copy-start | bytes 15364
  65.2 4.0 %copy-start.1 = (bf16[256,5120]{1,0:T(8,128)(2,1)S(1)}, bf16[256,5120]{1,0:T(8,128)(2,1)}, u32[]{:S(2)}) copy-start(bf16[256,5120]{1,0:T(8,128)(2,1)} %copy-done) | copy-start | bytes 7864324
  85.9 30.9 %copy-start.4 = (s32[32]{0:T(128)S(1)}, s32[32]{0:T(128)}, u32[]{:S(2)}) copy-start(s32[32]{0:T(128)} %param.14) | copy-start | bytes 388
  122.8 2.2 %copy-start.2 = (f32[256,4,5,128]{0,3,2,1:T(8,128)S(1)}, f32[256,4,5,128]{0,3,2,1:T(8,128)}, u32[]{:S(2)}) copy-start(f32[256,4,5,128]{0,3,2,1:T(8,128)} %get-tuple-element.387) | copy-start | bytes 7864324 | tf_op jit(solution)/shard_map/while
  127.8 1.5 copy-start.3
  135.3 2.2 %copy-start.2 = (f32[256,4,5,128]{0,3,2,1:T(8,128)S(1)}, f32[256,4,5,128]{0,3,2,1:T(8,128)}, u32[]{:S(2)}) copy-start(f32[256,4,5,128]{0,3,2,1:T(8,128)} %get-tuple-element.387) | copy-start | bytes 7864324 | tf_op jit(solution)/shard_map/while
  140.2 1.5 copy-start.3
  147.7 2.2 %copy-start.2 = (f32[256,4,5,128]{0,3,2,1:T(8,128)S(1)}, f32[256,4,5,128]{0,3,2,1:T(8,128)}, u32[]{:S(2)}) copy-start(f32[256,4,5,128]{0,3,2,1:T(8,128)} %get-tuple-element.387) | copy-start | bytes 7864324 | tf_op jit(solution)/shard_map/while
  152.7 1.5 copy-start.3
  160.2 2.2 %copy-start.2 = (f32[256,4,5,128]{0,3,2,1:T(8,128)S(1)}, f32[256,4,5,128]{0,3,2,1:T(8,128)}, u32[]{:S(2)}) copy-start(f32[256,4,5,128]{0,3,2,1:T(8,128)} %get-tuple-element.387) | copy-start | bytes 7864324 | tf_op jit(solution)/shard_map/while
  165.2 1.5 copy-start.3
Sparse Core Ops, SparseCore 0:
  9.0 36.3 all-gather.3
  58.3 28.2 all-gather.7
  88.2 28.5 all-gather.5

commit v2 on v0

v2 whole, which is shorter than its diff:
```python
import functools

import jax
import jax.numpy as jnp
from jax import lax
from jax.experimental import pallas as pl
from jax.experimental.pallas import tpu as pltpu
from jax.sharding import PartitionSpec as P

HD = 128
BLOCK = 64
THETA = 1000000.0
CUTS = 2
MESH = pl.DeviceIdType.MESH


def project_kernel(
    n,
    tp,
    pos_ref,
    place_ref,
    cos_ref,
    sin_ref,
    qb_ref,
    kb_ref,
    vb_ref,
    tok_hbm,
    clean_hbm,
    wq_hbm,
    wk_hbm,
    wv_hbm,
    q_out,
    k_out,
    v_out,
    tok,
    clean,
    wq,
    wk,
    wv,
    rows,
    posbuf,
    k_own,
    v_own,
    load_sem,
    zs,
    zr,
    ts,
    tr,
    cs,
    cr,
    ps,
    pr,
    kzs,
    kzr,
    kcs,
    kcr,
    own_sem,
):
    me = lax.axis_index("ctx")
    mine = lax.axis_index("tp")
    nz = n // 2
    z, c = me // 2, lax.rem(me, 2)
    right = lax.rem(z + 1, nz) * 2 + c
    left = lax.rem(z + nz - 1, nz) * 2 + c
    sib = z * 2 + 1 - c
    local, depth = tok.shape
    each = clean_hbm.shape[0]
    half = each // 2
    width = depth // tp
    kvw = wk.shape[1]
    qw = wq.shape[1]
    steps = nz - 1

    loads = [
        pltpu.make_async_copy(clean_hbm, rows.at[pl.ds(pl.multiple_of(me * each, each), each), :], load_sem.at[0]),
        pltpu.make_async_copy(tok_hbm, tok, load_sem.at[1]),
        pltpu.make_async_copy(wk_hbm, wk, load_sem.at[2]),
        pltpu.make_async_copy(wv_hbm, wv, load_sem.at[3]),
        pltpu.make_async_copy(wq_hbm, wq, load_sem.at[4]),
        pltpu.make_async_copy(clean_hbm, clean, load_sem.at[5]),
    ]
    loads[5].start()
    for load in loads[:5]:
        load.start()

    barrier = pltpu.get_barrier_semaphore()
    for k in range(1, n):
        pl.semaphore_signal(barrier, inc=1, device_id={"ctx": lax.rem(me + k, n)}, device_id_type=MESH)
    for k in range(1, tp):
        pl.semaphore_signal(barrier, inc=1, device_id={"tp": lax.rem(mine + k, tp)}, device_id_type=MESH)
    pl.semaphore_wait(barrier, n - 1 + tp - 1)

    def remote(src, dst, send, recv, where):
        return pltpu.make_async_remote_copy(
            src_ref=src, dst_ref=dst, send_sem=send, recv_sem=recv, device_id=where, device_id_type=MESH
        )

    started = []

    def go(copy):
        copy.start()
        started.append(copy)
        return copy

    own_columns = pl.ds(pl.multiple_of(mine * width, 128), width)

    def source(d, s):
        return lax.rem(z - s + nz, nz) * 2 + c if d == 0 else lax.rem(z + s, nz) * 2 + c

    def piece(block, d):
        return pl.ds(pl.multiple_of(block * each + d * half, half), half)

    loads[5].wait()
    for d in range(2):
        go(
            remote(
                clean.at[pl.ds(d * half, half), own_columns],
                rows.at[piece(me, d), own_columns],
                zs.at[d * steps],
                zr.at[d * steps],
                {"ctx": right if d == 0 else left},
            )
        )
    for k in range(1, n):
        go(remote(pos_ref, posbuf.at[me], ps.at[k - 1], pr.at[k - 1], {"ctx": lax.rem(me + k, n)}))
    own_core = go(
        remote(clean, rows.at[pl.ds(pl.multiple_of(me * each, each), each), :], cs.at[2 * steps], cr.at[2 * steps], {"ctx": sib})
    )
    posbuf[me] = pos_ref[...]

    core_copies = []

    def to_core(s):
        for d in range(2):
            region = rows.at[piece(source(d, s + 1), d), :]
            for k in range(1, tp):
                at = (d * steps + s) * (tp - 1) + k - 1
                part = rows.at[
                    piece(source(d, s + 1), d),
                    pl.ds(pl.multiple_of(lax.rem(mine + tp - k, tp) * width, 128), width),
                ]
                remote(part, part, ts.at[at], tr.at[at], {"tp": lax.rem(mine + k, tp)}).wait_recv()
            core_copies.append(go(remote(region, region, cs.at[d * steps + s], cr.at[d * steps + s], {"ctx": sib})))

    for s in range(steps):
        for d in range(2):
            part = rows.at[piece(source(d, s + 1), d), own_columns]
            where = {"ctx": right if d == 0 else left}
            at = d * steps + s
            remote(part, part, zs.at[at], zr.at[at], where).wait_recv()
            if s < steps - 1:
                go(remote(part, part, zs.at[at + 1], zr.at[at + 1], where))
            for k in range(1, tp):
                to = at * (tp - 1) + k - 1
                go(remote(part, part, ts.at[to], tr.at[to], {"tp": lax.rem(mine + k, tp)}))
        if s > 0:
            to_core(s - 1)
    to_core(steps - 1)
    own_core.wait_recv()
    for copy in core_copies:
        copy.wait_recv()
    for k in range(1, n):
        remote(pos_ref, posbuf.at[me], ps.at[k - 1], pr.at[k - 1], {"ctx": me}).wait_recv()
    loads[0].wait()
    loads[1].wait()

    everyone = jnp.max(posbuf[...], axis=0)[0:1, :]
    hits = place_ref[:, 0:1] == everyone
    chosen = jnp.where(hits, 1.0, 0.0).astype(jnp.bfloat16)
    present = jnp.max(jnp.where(hits, 1.0, 0.0), axis=1, keepdims=True) > 0.5
    span = 512

    def patch(j, carry):
        columns = pl.ds(pl.multiple_of(j * span, span), span)
        picked = jnp.dot(chosen, rows[:, columns], preferred_element_type=jnp.float32)
        tok[:, columns] = jnp.where(present, picked, tok[:, columns].astype(jnp.float32)).astype(jnp.bfloat16)
        return carry

    lax.fori_loop(0, depth // span, patch, 0)

    def project(weight, bias, out, rotated):
        total = weight.shape[1]
        tile = 256 if total % 256 == 0 else 128

        def one(j, carry):
            columns = pl.ds(pl.multiple_of(j * tile, tile), tile)
            result = jnp.dot(tok[...], weight[:, columns], preferred_element_type=jnp.float32)
            result = result + bias[:, columns].astype(jnp.float32)
            if rotated:
                parts = []
                for h in range(tile // HD):
                    head = result[:, h * HD : (h + 1) * HD]
                    parts.append(head * cos_ref[...] + pltpu.roll(head, HD // 2, 1) * sin_ref[...])
                result = jnp.concatenate(parts, axis=1) if len(parts) > 1 else parts[0]
            out[:, columns] = result.astype(jnp.bfloat16)
            return carry

        lax.fori_loop(0, total // tile, one, 0)

    cut = local // CUTS

    def slot(block, h):
        return pl.ds(pl.multiple_of(block * local + h * cut, cut), cut)

    def sem_at(d, s, h):
        return (d * nz + s) * CUTS + h

    outs = (k_out, v_out)
    owns = (k_own, v_own)
    own_copies = []

    def send_own(d):
        where = {"ctx": right if d == 0 else left}
        for h in range(CUTS):
            src = owns[d].at[pl.ds(h * cut, cut), :]
            dst = outs[d].at[slot(me, h), :]
            at = sem_at(d, 0, h)
            go(remote(src, dst, kzs.at[at], kzr.at[at], where))
        for h in range(CUTS):
            src = owns[d].at[pl.ds(h * cut, cut), :]
            dst = outs[d].at[slot(me, h), :]
            at = sem_at(d, steps, h)
            go(remote(src, dst, kcs.at[at], kcr.at[at], {"ctx": sib}))
        copy = pltpu.make_async_copy(owns[d], outs[d].at[pl.ds(pl.multiple_of(me * local, local), local), :], own_sem.at[d])
        copy.start()
        own_copies.append(copy)

    loads[2].wait()
    project(wk, kb_ref, k_own, True)
    send_own(0)
    loads[3].wait()
    project(wv, vb_ref, v_own, False)
    send_own(1)
    loads[4].wait()
    project(wq, qb_ref, q_out, True)

    for s in range(steps):
        for h in range(CUTS):
            for d in range(2):
                where = {"ctx": right if d == 0 else left}
                part = outs[d].at[slot(source(d, s + 1), h), :]
                at = sem_at(d, s, h)
                remote(part, part, kzs.at[at], kzr.at[at], where).wait_recv()
                if s < steps - 1:
                    then = sem_at(d, s + 1, h)
                    go(remote(part, part, kzs.at[then], kzr.at[then], where))
                go(remote(part, part, kcs.at[at], kcr.at[at], {"ctx": sib}))
    for s in range(nz):
        for h in range(CUTS):
            for d in range(2):
                at = sem_at(d, s, h)
                part = outs[d].at[slot(source(d, lax.rem(s + 1, nz)) + 1 - 2 * c, h), :]
                remote(part, part, kcs.at[at], kcr.at[at], {"ctx": sib}).wait_recv()
    for copy in own_copies:
        copy.wait()
    for copy in started:
        copy.wait_send()


def attend_kernel(kvh, group, inv_ref, lo_ref, blk_ref, q_ref, k_ref, v_ref, place_ref, start_ref, out_ref, qs, m_s, l_s, acc_s):
    i = pl.program_id(0)
    rows = group * BLOCK
    wide = 4
    keys = wide * BLOCK
    mine = blk_ref[i]
    low = lo_ref[i]
    for h in range(kvh):
        for g in range(group):
            head = h * group + g
            qs[h, g * BLOCK : (g + 1) * BLOCK, :] = q_ref[:, head * HD : (head + 1) * HD]
    m_s[...] = jnp.full_like(m_s, -1e30)
    l_s[...] = jnp.zeros_like(l_s)
    acc_s[...] = jnp.zeros_like(acc_s)
    places = place_ref[:, 0:1]
    starts = start_ref[:, 0:1]

    def step(t, carry):
        first = mine - wide * t - (wide - 1)
        at = [inv_ref[jnp.maximum(first + w, 0)] for w in range(wide)]
        at = [pl.multiple_of(a * BLOCK, BLOCK) for a in at]
        key_places = first * BLOCK + lax.broadcasted_iota(jnp.int32, (BLOCK, keys), 1)
        shown = (key_places >= starts) & (key_places <= places)
        shown = jnp.concatenate([jnp.where(shown, 1.0, 0.0)] * group, axis=0) > 0.5
        for h in range(kvh):
            head = slice(h * HD, (h + 1) * HD)
            k = jnp.concatenate([k_ref[pl.ds(a, BLOCK), head] for a in at], axis=0)
            v = jnp.concatenate([v_ref[pl.ds(a, BLOCK), head] for a in at], axis=0)
            scores = lax.dot_general(
                qs[h], k, (((1,), (1,)), ((), ())), preferred_element_type=jnp.float32
            ) * (HD**-0.5)
            scores = jnp.where(shown, scores, -1e30)
            old = m_s[h][:, 0:1]
            new = jnp.maximum(old, jnp.max(scores, axis=1, keepdims=True))
            factor = jnp.exp(old - new)
            weights = jnp.where(shown, jnp.exp(scores - new), 0.0)
            m_s[h] = jnp.broadcast_to(new, (rows, HD))
            l_s[h] = l_s[h] * factor + jnp.sum(weights, axis=1, keepdims=True)
            acc_s[h] = acc_s[h] * factor + jnp.dot(
                weights.astype(jnp.bfloat16), v, preferred_element_type=jnp.float32
            )
        return carry

    lax.fori_loop(0, (mine - low + wide) // wide, step, 0)
    for h in range(kvh):
        result = (acc_s[h] / l_s[h]).astype(jnp.bfloat16)
        for g in range(group):
            head = h * group + g
            out_ref[:, head * HD : (head + 1) * HD] = result[g * BLOCK : (g + 1) * BLOCK, :]


def body(n, tp, tokens, block_order, doc_lengths, patch_pos, clean_rows, w_query, q_bias, w_key, k_bias, w_value, v_bias):
    local, depth = tokens.shape
    each = patch_pos.shape[0]
    patches = each * n
    qw, kvw = w_query.shape[1], w_key.shape[1]
    kvh = kvw // HD
    group = qw // kvw
    blocks = local // BLOCK
    me = lax.axis_index("ctx")
    nz = n // 2

    ids = jnp.arange(block_order.shape[0], dtype=jnp.int32)
    own_blocks = lax.dynamic_slice(block_order, (me * blocks,), (blocks,))
    inverse = jnp.sum(jnp.where(block_order[None, :] == ids[:, None], ids[None, :], 0), axis=1)
    places = (own_blocks[:, None] * BLOCK + jnp.arange(BLOCK, dtype=jnp.int32)[None, :]).reshape(local)
    index = jnp.arange(doc_lengths.shape[0], dtype=jnp.int32)
    bounds = jnp.sum(jnp.where(index[:, None] <= index[None, :], doc_lengths[:, None], 0), axis=0)
    passed = places[:, None] >= bounds[None, :]
    starts = jnp.sum(jnp.where(passed, doc_lengths[None, :], 0), axis=1)
    offset = places - starts
    lowest = starts.reshape(blocks, BLOCK)[:, 0] // BLOCK
    frequency = jnp.power(jnp.float32(THETA), -2.0 * jnp.arange(HD // 2, dtype=jnp.float32) / HD)
    angles = offset.astype(jnp.float32)[:, None] * frequency[None, :]
    cosines, sines = jnp.cos(angles), jnp.sin(angles)
    cos_all = jnp.concatenate([cosines, cosines], axis=1)
    sin_all = jnp.concatenate([-sines, sines], axis=1)
    place_wide = jnp.broadcast_to(places[:, None], (local, HD))
    start_wide = jnp.broadcast_to(starts[:, None], (local, HD))
    lane = jnp.arange(patches, dtype=jnp.int32)
    pos_row = jnp.where(lane // each == me, jnp.tile(patch_pos, n), -1)
    pos_wide = jnp.broadcast_to(pos_row[None, :], (8, patches))

    vmem = pl.BlockSpec(memory_space=pltpu.VMEM)
    hbm = pl.BlockSpec(memory_space=pl.ANY)
    dma = pltpu.SemaphoreType.DMA
    steps = nz - 1
    query, keys, values = pl.pallas_call(
        functools.partial(project_kernel, n, tp),
        out_shape=(
            jax.ShapeDtypeStruct((local, qw), jnp.bfloat16),
            jax.ShapeDtypeStruct((n * local, kvw), jnp.bfloat16),
            jax.ShapeDtypeStruct((n * local, kvw), jnp.bfloat16),
        ),
        in_specs=[vmem] * 7 + [hbm] * 5,
        out_specs=(vmem, hbm, hbm),
        scratch_shapes=[
            pltpu.VMEM((local, depth), jnp.bfloat16),
            pltpu.VMEM((each, depth), jnp.bfloat16),
            pltpu.VMEM((depth, qw), jnp.bfloat16),
            pltpu.VMEM((depth, kvw), jnp.bfloat16),
            pltpu.VMEM((depth, kvw), jnp.bfloat16),
            pltpu.VMEM((patches, depth), jnp.bfloat16),
            pltpu.VMEM((n, 8, patches), jnp.int32),
            pltpu.VMEM((local, kvw), jnp.bfloat16),
            pltpu.VMEM((local, kvw), jnp.bfloat16),
            dma((6,)),
            dma((2 * steps,)),
            dma((2 * steps,)),
            dma((2 * steps * (tp - 1),)),
            dma((2 * steps * (tp - 1),)),
            dma((2 * steps + 1,)),
            dma((2 * steps + 1,)),
            dma((n - 1,)),
            dma((n - 1,)),
            dma((2 * nz * CUTS,)),
            dma((2 * nz * CUTS,)),
            dma((2 * nz * CUTS,)),
            dma((2 * nz * CUTS,)),
            dma((2,)),
        ],
        compiler_params=pltpu.CompilerParams(
            collective_id=0, has_side_effects=True, vmem_limit_bytes=58 * 1024 * 1024
        ),
        cost_estimate=pl.CostEstimate(
            flops=2 * local * depth * (qw + 2 * kvw), bytes_accessed=2 * depth * (qw + 2 * kvw), transcendentals=0
        ),
    )(
        pos_wide,
        place_wide,
        cos_all,
        sin_all,
        q_bias[None, :],
        k_bias[None, :],
        v_bias[None, :],
        tokens,
        clean_rows,
        w_query,
        w_key,
        w_value,
    )

    whole = lambda i, *_: (0, 0)
    part = lambda i, *_: (i, 0)
    return pl.pallas_call(
        functools.partial(attend_kernel, kvh, group),
        out_shape=jax.ShapeDtypeStruct((local, qw), jnp.bfloat16),
        grid_spec=pltpu.PrefetchScalarGridSpec(
            num_scalar_prefetch=3,
            grid=(blocks,),
            in_specs=[
                pl.BlockSpec((BLOCK, qw), part),
                pl.BlockSpec((n * local, kvw), whole),
                pl.BlockSpec((n * local, kvw), whole),
                pl.BlockSpec((BLOCK, HD), part),
                pl.BlockSpec((BLOCK, HD), part),
            ],
            out_specs=pl.BlockSpec((BLOCK, qw), part),
            scratch_shapes=[
                pltpu.VMEM((kvh, group * BLOCK, HD), jnp.bfloat16),
                pltpu.VMEM((kvh, group * BLOCK, HD), jnp.float32),
                pltpu.VMEM((kvh, group * BLOCK, HD), jnp.float32),
                pltpu.VMEM((kvh, group * BLOCK, HD), jnp.float32),
            ],
        ),
        compiler_params=pltpu.CompilerParams(vmem_limit_bytes=40 * 1024 * 1024),
        cost_estimate=pl.CostEstimate(flops=10**9, bytes_accessed=6 * 10**6, transcendentals=10**6),
    )(inverse, lowest, own_blocks, query, keys, values, place_wide, start_wide)


def solution(mesh):
    in_specs = (
        P(("run", "ctx"), None),
        P(),
        P(),
        P(("run", "ctx")),
        P(("run", "ctx"), None),
        P(None, "tp"),
        P("tp"),
        P(None, "tp"),
        P("tp"),
        P(None, "tp"),
        P("tp"),
    )
    out_specs = P(("run", "ctx"), "tp")
    return jax.shard_map(
        functools.partial(body, mesh.shape["ctx"], mesh.shape["tp"]),
        mesh=mesh,
        in_specs=in_specs,
        out_specs=out_specs,
        check_vma=False,
    )
```

time: 177 us -> 105 us (0.59)
  the two profiles are of different devices: /device:TPU:1 before, /device:TPU:9 now
where the time goes in v2:
time: 105 us
  Pallas kernels  89.3 us (85%)
  local copies, waits for them, and re-layouts  10.8 us (10%)
  other arithmetic  4.5 us (4%)
    pallas_call x1, Pallas kernels, body(): pl.pallas_call(functools.partial(project_kernel, n, tp), out_shape=(jax.S...  68.7 us
    pallas_call x1, Pallas kernels, body(): pl.pallas_call(functools.partial(attend_kernel, kvh, group), out_shape=ja...  20.5 us
    unnamed x8, local copies, waits for them, and re-layouts  4.49 us

profile of v2, /device:TPU:9, one launch (start us, length us, event | category | flops | bytes accessed | tf_op | source)
XLA Modules:
  0.0 104.6 jit_solution(17682107608233303746)
XLA Ops:
  0.0 0.8 select_reduce_fusion.1.inv_ref
  0.8 0.7 select_reduce_fusion.2
  1.5 0.7 broadcast_multiply_fusion
  2.3 0.1 iota_add_fusion
  2.3 0.1 add.37
  2.4 0.7 select_reduce_fusion
  3.2 0.1 reshape.62
  3.2 0.1 slice_reduce_fusion
  3.4 1.3 %broadcast_in_dim.85.kb_ref = bf16[1,512]{1,0:T(2,128)(2,1)} reshape(bf16[512]{0:T(512)(128)(2,1)} %param.19) | data formatting | bytes 2048 | tf_op jit(solution)/shard_map/broadcast_in_dim | solution.py:393
  4.7 1.3 %broadcast_in_dim.86.vb_ref = bf16[1,512]{1,0:T(2,128)(2,1)} reshape(bf16[512]{0:T(512)(128)(2,1)} %param.21) | data formatting | bytes 2048 | tf_op jit(solution)/shard_map/broadcast_in_dim | solution.py:394
  5.9 0.7 tile.4
  6.6 0.1 tile.10
  6.7 0.6 broadcast_in_dim.82.pos_ref
  7.3 1.3 %broadcast_in_dim.84.qb_ref = bf16[1,2560]{1,0:T(2,128)(2,1)} reshape(bf16[2560]{0:T(1024)(128)(2,1)} %param.17) | data formatting | bytes 10240 | tf_op jit(solution)/shard_map/broadcast_in_dim | solution.py:392
  8.6 0.8 broadcast_in_dim.83.place_ref
  9.3 0.1 broadcast_in_dim.87.start_ref
  9.4 0.5 fusion
  10.0 0.9 pad_maximum_fusion
  10.8 68.7 %shard_map.109 = (bf16[256,2560]{1,0:T(8,128)(2,1)}, bf16[2048,512]{1,0:T(8,128)(2,1)}, bf16[2048,512]{1,0:T(8,128)(2,1)}) custom-call(s32[8,256]{1,0:T(8,128)} %broadcast_in_dim.82.pos_ref, s32[256,128]{1,0:T(8,128)} %broadcast_in_dim.83.place_ref, f32[256,128]{1,0:T(8,128)} %get-tuple-element.16.cos_ref, f32[256,128]{1,0:T(8,128)} %get-tuple-element.17.sin_ref, ...), custom_call_target="tpu_custom_call" | custom-call | flops 9395240960 | bytes 36700160 | tf_op jit(solution)/shard_map/pallas_call | solution.py:347
  79.5 0.0 copy-done.3
  79.6 1.6 %copy-done = bf16[2048,512]{1,0:T(8,128)(2,1)S(1)} copy-done((bf16[2048,512]{1,0:T(8,128)(2,1)S(1)}, bf16[2048,512]{1,0:T(8,128)(2,1)}, u32[]{:S(2)}) %copy-start) | copy-done | bytes 2097176
  81.1 1.6 %copy-done.1 = bf16[2048,512]{1,0:T(8,128)(2,1)S(1)} copy-done((bf16[2048,512]{1,0:T(8,128)(2,1)S(1)}, bf16[2048,512]{1,0:T(8,128)(2,1)}, u32[]{:S(2)}) %copy-start.1) | copy-done | bytes 2097176
  82.7 1.3 %copy-done.2 = bf16[256,2560]{1,0:T(8,128)(2,1)S(1)} copy-done((bf16[256,2560]{1,0:T(8,128)(2,1)S(1)}, bf16[256,2560]{1,0:T(8,128)(2,1)}, u32[]{:S(2)}) %copy-start.2) | copy-done | bytes 1310744
  84.1 20.5 %shard_map.110 = bf16[256,2560]{1,0:T(8,128)(2,1)} custom-call(s32[32]{0:T(128)S(1)} %select_reduce_fusion.1.inv_ref, s32[4]{0:T(128)S(1)} %and_select_fusion.1.lo_ref, s32[4]{0:T(128)S(1)} %get-tuple-element.12.blk_ref, bf16[256,2560]{1,0:T(8,128)(2,1)S(1)} %copy-done.2, bf16[2048,512]{1,0:T(8,128)(2,1)S(1)} %copy-done, bf16[2048,512]{1,0:T(8,128)(2,1)S(1)} %copy-done.1, ...), custom_call_target="tpu_custom_call" | custom-call | flops 1000000000 | bytes 6000000 | tf_op jit(solution)/shard_map/pallas_call | solution.py:404
  (8 shorter events, 0.0 us)
Async XLA Ops:
  10.8 68.7 %copy-start.3 = (s32[256,128]{1,0:T(8,128)S(1)}, s32[256,128]{1,0:T(8,128)}, u32[]{:S(2)}) copy-start(s32[256,128]{1,0:T(8,128)} %broadcast_in_dim.83.place_ref) | copy-start | bytes 393220
  79.6 1.6 %copy-start = (bf16[2048,512]{1,0:T(8,128)(2,1)S(1)}, bf16[2048,512]{1,0:T(8,128)(2,1)}, u32[]{:S(2)}) copy-start(bf16[2048,512]{1,0:T(8,128)(2,1)} %get-tuple-element.9.k_ref) | copy-start | bytes 6291460
  81.1 1.6 %copy-start.1 = (bf16[2048,512]{1,0:T(8,128)(2,1)S(1)}, bf16[2048,512]{1,0:T(8,128)(2,1)}, u32[]{:S(2)}) copy-start(bf16[2048,512]{1,0:T(8,128)(2,1)} %get-tuple-element.10.v_ref) | copy-start | bytes 6291460
  82.7 1.3 %copy-start.2 = (bf16[256,2560]{1,0:T(8,128)(2,1)S(1)}, bf16[256,2560]{1,0:T(8,128)(2,1)}, u32[]{:S(2)}) copy-start(bf16[256,2560]{1,0:T(8,128)(2,1)} %get-tuple-element.8.q_ref) | copy-start | bytes 3932164
